TPU v7x, 128 devices: a whole 4x4x4 slice. The times are simulated.
128 devices in a mesh: dev: 128 (over y, z, x, core).
Axes of the slice: x: 4, y: 4, z: 4, core: 2. Of those that a mesh axis runs over, the one named last changes fastest.
Arguments:
- upstream: bfloat16 [65536, 1024], P('dev'), may hold values from -24 to 24
- bag: int32 [65536, 8], P('dev'), may hold values from 0 to 767
- next_bag: int32 [65536, 8], P('dev'), may hold values from 0 to 511
- hot_slots: int32 [65536], P('dev'), may hold values from 0 to 8191, as said below
- evict_dest: int32 [128, 128, 2], P('dev'), may hold values from -1 to 1023, as said below
- hot_cache: float32 [65536, 128], P('dev'), may hold values from -6 to 6
- evict_cache: float32 [32768, 128], P('dev'), may hold values from -6 to 6
- hot_table: float32 [8192, 128], P('dev'), may hold values from -6 to 6
- hot_accum: float32 [8192, 128], P('dev'), may hold values from 1 to 100
- owner_table: float32 [131072, 128], P('dev'), may hold values from -6 to 6
- owner_accum: float32 [131072, 128], P('dev'), may hold values from 1 to 30
- cross_w: float32 [2, 1024, 1024], P(None, None, 'dev'), may hold values from -0.1875 to 0.1875
- cross_b: float32 [2, 1024], P(None, 'dev'), may hold values from -3 to 3
- cross_accum: float32 [2, 1024, 1024], P(None, None, 'dev'), may hold values from 10000 to 1000000
Outputs:
- next_first: bfloat16 [65536, 1024], P('dev')
- hot_new: float32 [8192, 128], P('dev')
- hot_accum_new: float32 [8192, 128], P('dev')
- owner_new: float32 [131072, 128], P('dev')
- owner_accum_new: float32 [131072, 128], P('dev')
- cross_w_new: float32 [2, 1024, 1024], P(None, None, 'dev')
- cross_b_new: float32 [2, 1024], P(None, 'dev')
Inputs may be any that keep to these rules, and one draw needn't show every extreme that they name: `hot_slots`: entry d * 512 + 4 * o + k names a row of owner o's block, o * 64 to o * 64 + 63; the 4 rows of one device in one owner's block are distinct. evict_dest[o, s, k] is the row of owner o's block (0 to 1023) that receives the gradient of source s's evicted slot 2 * o + k, or -1 for an empty slot; in each (o, s) bucket the live entries come first, and some bucket is full in every draw.
All inputs are finite; a program needn't handle non-finite values.
Results may differ from a plain program's by a relative error of at most 0.0033.
The roundings to bfloat16 on the way count: a program that leaves them out, or rounds other values in their place, can miss the bound.
Values may be sent and summed in bfloat16 or wider, within the bound.
A program may use at most 128 MiB of HBM per device.

v0:
```python
import jax
import jax.numpy as jnp
from jax import lax
from jax.sharding import PartitionSpec as P

row_rate = 0.05
weight_rate = 0.005
bias_rate = 0.0002
epsilon = 1e-10


def rows_first(arrays, axis, dims):
    turned = [jnp.moveaxis(a, dim, 0) for a, dim in zip(arrays, dims)]
    both = jnp.concatenate([t.reshape(len(t), -1) for t in turned], axis=1)
    filled, at, gathered = (lax.all_gather(both, axis, axis=0, tiled=True), 0, [])
    for t, dim in zip(turned, dims):
        piece = filled[:, at : at + t[0].size].reshape(-1, *t.shape[1:])
        gathered.append(jnp.moveaxis(piece, 0, dim))
        at += t[0].size
    return tuple(gathered)


def adagrad(params, accumulator, gradient, step_rate):
    updated = accumulator + gradient * gradient
    return (params - step_rate * gradient / (jnp.sqrt(updated) + epsilon), updated)


def owner_update(moved, evict_dest, owner_table, owner_accum, width):
    destination = evict_dest[0]
    targets = jnp.where(destination >= 0, destination, owner_table.shape[0]).reshape(-1)
    owner_grad = (
        jnp.zeros(owner_table.shape, jnp.float32)
        .at[targets]
        .add(moved.reshape(-1, width), mode="drop")
    )
    return adagrad(owner_table, owner_accum, owner_grad, row_rate)


def shared_update(arrived_ids, arrived, my_index, hot_table, hot_accum, devices, width):
    block_rows = hot_table.shape[0]
    local_rows = (arrived_ids - my_index * block_rows).reshape(-1)
    block_grad = (
        jnp.zeros(hot_table.shape, jnp.float32).at[local_rows].add(arrived.reshape(-1, width))
    )
    hot_new, hot_accum_new = adagrad(hot_table, hot_accum, block_grad, row_rate)
    returned = jnp.take(hot_new, local_rows, axis=0).reshape(devices, -1, width)
    return (hot_new, hot_accum_new, returned)


def local(
    upstream,
    bag,
    next_bag,
    hot_slots,
    evict_dest,
    hot_cache,
    evict_cache,
    hot_table,
    hot_accum,
    owner_table,
    owner_accum,
    cross_w,
    cross_b,
    cross_accum,
):
    devices = lax.axis_size("dev")
    my_index = lax.axis_index("dev")
    width = hot_cache.shape[1]
    samples = bag.shape[0]
    hot_count = hot_cache.shape[0]
    weights, biases = rows_first(
        (cross_w.astype(jnp.bfloat16), cross_b.astype(jnp.bfloat16)), "dev", (2, 1)
    )
    biases = biases.astype(jnp.float32)
    slot_values = jnp.concatenate([hot_cache, evict_cache], axis=0)
    slot_total = slot_values.shape[0]
    features = jnp.take(slot_values, bag.reshape(-1), axis=0).reshape(samples, -1)
    feat_bf = features.astype(jnp.bfloat16)
    proj_one = jnp.dot(feat_bf, weights[0], preferred_element_type=jnp.float32) + biases[0]
    layer_one = features * proj_one + features
    layer_bf = layer_one.astype(jnp.bfloat16)
    proj_two = jnp.dot(layer_bf, weights[1], preferred_element_type=jnp.float32) + biases[1]
    grad_out = upstream.astype(jnp.float32)
    grad_two = grad_out * features
    grad_two_bf = grad_two.astype(jnp.bfloat16)
    weight_two = jnp.dot(layer_bf.T, grad_two_bf, preferred_element_type=jnp.float32)
    bias_two = jnp.sum(grad_two, axis=0)
    grad_layer = grad_out + jnp.dot(grad_two_bf, weights[1].T, preferred_element_type=jnp.float32)
    grad_one = grad_layer * features
    grad_one_bf = grad_one.astype(jnp.bfloat16)
    weight_one = jnp.dot(feat_bf.T, grad_one_bf, preferred_element_type=jnp.float32)
    bias_one = jnp.sum(grad_one, axis=0)
    weight_shard, bias_shard = (
        lax.psum_scatter(
            jnp.stack([weight_one, weight_two]), "dev", scatter_dimension=2, tiled=True
        ),
        lax.psum_scatter(jnp.stack([bias_one, bias_two]), "dev", scatter_dimension=1, tiled=True),
    )
    grad_feat = grad_out * proj_two + grad_layer * (proj_one + 1.0)
    grad_feat = grad_feat + jnp.dot(grad_one_bf, weights[0].T, preferred_element_type=jnp.float32)
    grad_rows = grad_feat.astype(jnp.bfloat16).reshape(-1, width)
    one_hot = (
        bag.reshape(-1)[:, None]
        == lax.broadcasted_iota(jnp.int32, (grad_rows.shape[0], slot_total), 1)
    ).astype(jnp.bfloat16)
    slot_grad = lax.dot_general(
        one_hot, grad_rows, (((0,), (0,)), ((), ())), preferred_element_type=jnp.float32
    )
    hot_grads = slot_grad[:hot_count].reshape(devices, -1, width)
    evict_grads = slot_grad[hot_count:].reshape(devices, -1, width)
    shared_per = hot_grads.shape[1]
    arrived_ids = lax.all_to_all(
        hot_slots.reshape(devices, -1), "dev", split_axis=0, concat_axis=0, tiled=True
    )
    packed = jnp.concatenate([hot_grads, evict_grads], axis=1)
    unpacked = lax.all_to_all(packed, "dev", split_axis=0, concat_axis=0, tiled=True)
    arrived = unpacked[:, :shared_per]
    moved = unpacked[:, shared_per:]
    hot_new, hot_accum_new, returned = shared_update(
        arrived_ids, arrived, my_index, hot_table, hot_accum, devices, width
    )
    held_rows = lax.all_to_all(returned, "dev", split_axis=0, concat_axis=0, tiled=True).reshape(
        hot_count, width
    )
    owner_new, owner_accum_new = owner_update(moved, evict_dest, owner_table, owner_accum, width)
    cross_w_new, unused = adagrad(cross_w, cross_accum, weight_shard, weight_rate)
    cross_b_new = cross_b - bias_rate * bias_shard
    first_weight, first_bias = rows_first(
        (cross_w_new[0].astype(jnp.bfloat16), cross_b_new[0].astype(jnp.bfloat16)), "dev", (1, 0)
    )
    next_feat = jnp.take(held_rows, next_bag.reshape(-1), axis=0).reshape(next_bag.shape[0], -1)
    proj = jnp.dot(
        next_feat.astype(jnp.bfloat16), first_weight, preferred_element_type=jnp.float32
    ) + first_bias.astype(jnp.float32)
    next_first = (next_feat * proj + next_feat).astype(jnp.bfloat16)
    return (
        next_first,
        hot_new,
        hot_accum_new,
        owner_new,
        owner_accum_new,
        cross_w_new,
        cross_b_new,
    )


def solution(mesh):
    return jax.shard_map(
        local,
        mesh=mesh,
        in_specs=(
            P("dev", None),
            P("dev", None),
            P("dev", None),
            P("dev"),
            P("dev", None, None),
            P("dev", None),
            P("dev", None),
            P("dev", None),
            P("dev", None),
            P("dev", None),
            P("dev", None),
            P(None, None, "dev"),
            P(None, "dev"),
            P(None, None, "dev"),
        ),
        out_specs=(
            P("dev", None),
            P("dev", None),
            P("dev", None),
            P("dev", None),
            P("dev", None),
            P(None, None, "dev"),
            P(None, "dev"),
        ),
        check_vma=False,
    )
```

profile of v0, /device:TPU:1, one launch (start us, length us, event | category | flops | bytes accessed | tf_op | source)
XLA Modules:
  0.0 369.3 jit_solution(14683335172058845515)
XLA Ops:
  11.7 14.1 %gather_fusion = f32[4096,128]{1,0:T(8,128)} fusion(f32[768,128]{1,0:T(8,128)S(1)} %pad_maximum_fusion.2, s32[4096]{0:T(1024)S(1)} %broadcast_clamp_fusion.1), kind=kCustom, calls=%fused_computation | custom fusion | bytes 4210688 | tf_op jit(solution)/shard_map/jit(_take)/gather | solution.py:77
  25.7 1.7 gather.21
  27.7 2.7 fusion.9
  30.4 51.9 %all-gather.3.cloned.1.call-done = bf16[1024,2050]{1,0:T(8,128)(2,1)} async-done(((bf16[8,2050]{1,0:T(8,128)(2,1)}), bf16[1024,2050]{1,0:T(8,128)(2,1)}) %all-gather.3.cloned.1.call-update) | async-done | bytes 4198416 | tf_op jit(solution)/shard_map/all_gather | solution.py:15
  82.3 4.8 %slice.66 = bf16[1024,2048]{1,0:T(8,128)(2,1)} slice(bf16[1024,2050]{1,0:T(8,128)(2,1)} %all-gather.3.cloned.1.call-done), slice={[0:1024], [0:2048]} | slice | bytes 8388608 | tf_op jit(solution)/shard_map/slice | solution.py:17
  87.1 6.4 %copy.92 = bf16[1024,2048]{0,1:T(8,128)(2,1)} copy(bf16[1024,2048]{1,0:T(8,128)(2,1)} %slice.66) | data formatting | bytes 8388608 | tf_op jit(solution)/shard_map/reshape | solution.py:17
  95.0 3.3 fusion.11
  98.3 1.6 broadcast_in_dim.51
  100.0 1.7 multiply_reduce_fusion
  101.6 1.4 convolution_bitcast_fusion.1
  103.0 1.7 convolution_bitcast_fusion
  104.7 4.1 %pad_maximum_fusion = f32[2,1024,1024]{2,1,0:T(8,128)} fusion(f32[1,1024,1024]{2,1,0:T(8,128)S(1)} %convolution_bitcast_fusion, f32[1,1024,1024]{2,1,0:T(8,128)S(1)} %convolution_bitcast_fusion.1), kind=kLoop, calls=%fused_computation.7 | loop fusion | flops 2097152 | bytes 16777216 | tf_op jit(solution)/shard_map/stack | solution.py:95
  108.8 13.4 %copy.86 = f32[2,1024,1024]{1,0,2:T(2,128)} copy(f32[2,1024,1024]{2,1,0:T(8,128)} %pad_maximum_fusion) | data formatting | bytes 16777216 | tf_op jit(solution)/shard_map/stack | solution.py:95
  123.6 5.4 %all-to-all-start = ((s32[128,1,4]{2,1,0:T(1,128)}), s32[128,1,4]{2,1,0:T(1,128)S(1)}, u32[]{:S(2)}, u32[]{:S(2)}) async-start(s32[128,1,4]{2,1,0:T(1,128)} %bitcast), calls=%async_computation | async-start | bytes 131072 | tf_op jit(solution)/shard_map/all_to_all | solution.py:112
  129.4 68.7 %all-reduce.1 = f32[2,1024]{1,0:T(2,128)S(1)} all-reduce(f32[2,1024]{1,0:T(2,128)S(1)} %pad_maximum_fusion.5), channel_id=3, replica_groups=mesh['dev'=128] {'dev'}, use_global_device_ids=true, to_apply=%region_4.5.clone | all-reduce | flops 2048 | bytes 16384
  198.8 82.2 %all-reduce.4.cloned.1.call-done = f32[2,1024,1024]{1,0,2:T(2,128)} async-done(((f32[2,1024,1024]{1,0,2:T(2,128)}), f32[2,1024,1024]{1,0,2:T(2,128)}) %all-reduce.4.cloned.1.call-update) | async-done | bytes 8388624
  284.8 3.7 fusion.10
  289.1 4.9 %fusion.4 = bf16[512,1024]{1,0:T(8,128)(2,1)} fusion(f32[512,1024]{1,0:T(8,128)S(1)} %fusion.10, bf16[512,1024]{1,0:T(8,128)(2,1)S(1)} %copy-done.18, f32[512,1024]{1,0:T(8,128)S(1)} %copy-done.4, f32[512,1024]{1,0:T(8,128)} %copy-done.19, bf16[2,1024,1024]{2,1,0:T(8,128)(2,1)S(1)} %bitcast.104, f32[1024]{0:T(1024)S(1)} %get-tuple-element.38, ...), kind=kOutput, calls=%fused_computation.18 | convolution fusion | flops 1081081856 | bytes 15216640 | tf_op jit(solution)/shard_map/dot_general | solution.py:82
  294.0 1.5 reshape.231
  295.6 4.0 %fusion = f32[768,128]{1,0:T(8,128)S(1)} fusion(bf16[4096,128]{1,0:T(8,128)(2,1)S(1)} %reshape.231, s32[4096]{0:T(1024)S(1)} %eq.10), kind=kOutput, calls=%fused_computation.6 | convolution fusion | flops 808452096 | bytes 1458176 | tf_op jit(solution)/shard_map/dot_general | solution.py:106
  300.6 6.6 %all-to-all-start.1 = ((f32[128,6,128]{2,1,0:T(8,128)}), f32[128,6,128]{2,1,0:T(8,128)S(1)}, u32[]{:S(2)}, u32[]{:S(2)}) async-start(f32[128,6,128]{2,1,0:T(8,128)} %pad_maximum_fusion.1), calls=%async_computation.1 | async-start | bytes 1048576 | tf_op jit(solution)/shard_map/all_to_all | solution.py:116
  307.3 13.7 %all-to-all-done.1 = f32[128,6,128]{2,1,0:T(8,128)S(1)} async-done(((f32[128,6,128]{2,1,0:T(8,128)}), f32[128,6,128]{2,1,0:T(8,128)S(1)}, u32[]{:S(2)}, u32[]{:S(2)}) %all-to-all-start.1) | async-done | bytes 393248 | tf_op jit(solution)/shard_map/all_to_all | solution.py:116
  321.0 2.3 scatter_custom_fusion
  325.9 4.6 %all-to-all-start.2 = ((f32[128,4,128]{2,1,0:T(4,128)}), f32[128,4,128]{2,1,0:T(4,128)S(1)}, u32[]{:S(2)}, u32[]{:S(2)}) async-start(f32[128,4,128]{2,1,0:T(4,128)} %broadcast_select_fusion), calls=%async_computation.2 | async-start | bytes 524288 | tf_op jit(solution)/shard_map/all_to_all | solution.py:122
  330.5 1.6 scatter_custom_fusion.1
  332.1 1.2 divide_subtract_fusion
  333.3 9.2 %all-to-all-done.2 = f32[128,4,128]{2,1,0:T(4,128)S(1)} async-done(((f32[128,4,128]{2,1,0:T(4,128)}), f32[128,4,128]{2,1,0:T(4,128)S(1)}, u32[]{:S(2)}, u32[]{:S(2)}) %all-to-all-start.2) | async-done | bytes 262176 | tf_op jit(solution)/shard_map/all_to_all | solution.py:122
  342.5 10.8 %gather_fusion.2 = f32[4096,128]{1,0:T(8,128)S(1)} fusion(f32[512,128]{1,0:T(8,128)S(1)} %bitcast.95, s32[4096]{0:T(1024)S(1)} %broadcast_clamp_fusion), kind=kCustom, calls=%fused_computation.2 | custom fusion | bytes 4210688 | tf_op jit(solution)/shard_map/jit(_take)/gather | solution.py:131
  353.3 1.5 gather.26
  354.7 1.1 convert_reduce_fusion
  355.8 1.6 broadcast_in_dim.47
  357.5 5.3 %fusion.6 = bf16[512,1024]{1,0:T(8,128)(2,1)} fusion(f32[512,1024]{1,0:T(8,128)} %gather.26, pred[64,8,8,128]{3,2,1,0:T(8,128)(4,1)S(1)} %bitcast.109, bf16[1024,1025]{1,0:T(8,128)(2,1)} %all-gather.5.cloned.1.call-done, f32[1024]{0:T(1024)S(1)} %convert_reduce_fusion), kind=kOutput, calls=%fused_computation.20 | convolution fusion | flops 1077411840 | bytes 8392704 | tf_op jit(solution)/shard_map/dot_general | solution.py:132
  (94 shorter events, 16.5 us)
Async XLA Ops:
  7.2 75.1 %all-gather.3.cloned.1.call-start = ((), (), s32[]{:S(2)}) async-start(), calls=%async_computation.3 | async-start | bytes 4491264 | tf_op jit(solution)/shard_map/all_gather | solution.py:15
  9.5 271.6 %all-reduce.4.cloned.1.call-start = ((), (), s32[]{:S(2)}) async-start(), calls=%async_computation.5 | async-start | bytes 16777216
  25.7 1.7 copy-start.9
  95.0 5.0 %copy-start.1 = (bf16[1024,2048]{0,1:T(8,128)(2,1)S(1)}, bf16[1024,2048]{0,1:T(8,128)(2,1)}, u32[]{:S(2)}) copy-start(bf16[1024,2048]{0,1:T(8,128)(2,1)} %copy.92) | copy-start | bytes 12582916
  95.0 5.0 %copy-start.17 = (bf16[512,1024]{1,0:T(8,128)(2,1)S(1)}, bf16[512,1024]{1,0:T(8,128)(2,1)}, u32[]{:S(2)}) copy-start(bf16[512,1024]{1,0:T(8,128)(2,1)} %param.14) | copy-start | bytes 3145732
  98.3 4.7 %copy-start.19 = (f32[512,1024]{1,0:T(8,128)}, f32[512,1024]{1,0:T(8,128)S(1)}, u32[]{:S(2)}) copy-start(f32[512,1024]{1,0:T(8,128)S(1)} %fusion.11) | copy-start | bytes 6291460
  101.6 1.4 copy-start.3
  122.2 0.7 copy-start.14
  122.2 6.9 %copy-start.10 = (s32[512,8]{0,1:T(8,128)S(1)}, s32[512,8]{0,1:T(8,128)}, u32[]{:S(2)}) copy-start(s32[512,8]{0,1:T(8,128)} %param.16) | copy-start | bytes 49156
  122.2 75.9 %copy-start.16 = (f32[2,8]{1,0:T(2,128)S(1)}, f32[2,8]{1,0:T(2,128)}, u32[]{:S(2)}) copy-start(f32[2,8]{1,0:T(2,128)} %param.26) | copy-start | bytes 196
  122.2 159.7 %copy-start.7 = (f32[2,1024,8]{1,2,0:T(8,128)S(1)}, f32[2,1024,8]{1,2,0:T(8,128)}, u32[]{:S(2)}) copy-start(f32[2,1024,8]{1,2,0:T(8,128)} %param.25) | copy-start | bytes 196612
  122.2 159.7 %copy-start.11 = (f32[2,1024,8]{1,2,0:T(8,128)S(1)}, f32[2,1024,8]{1,2,0:T(8,128)}, u32[]{:S(2)}) copy-start(f32[2,1024,8]{1,2,0:T(8,128)} %param.27) | copy-start | bytes 196612
  122.2 160.4 %copy-start.15 = (s32[1,128,2]{1,2,0:T(2,128)S(1)}, s32[1,128,2]{1,2,0:T(2,128)}, u32[]{:S(2)}) copy-start(s32[1,128,2]{1,2,0:T(2,128)} %param.18) | copy-start | bytes 3076
  123.6 159.7 %all-to-all-start = ((s32[128,1,4]{2,1,0:T(1,128)}), s32[128,1,4]{2,1,0:T(1,128)S(1)}, u32[]{:S(2)}, u32[]{:S(2)}) async-start(s32[128,1,4]{2,1,0:T(1,128)} %bitcast), calls=%async_computation | async-start | bytes 131072 | tf_op jit(solution)/shard_map/all_to_all | solution.py:112
  129.0 225.7 %all-gather.5.cloned.1.call-start = ((), (), s32[]{:S(2)}) async-start(), calls=%async_computation.4 | async-start | bytes 2377728 | tf_op jit(solution)/shard_map/all_gather | solution.py:15
  282.0 6.5 %copy-start.8 = (f32[2,1024,8]{1,2,0:T(8,128)}, f32[2,1024,8]{1,2,0:T(8,128)S(1)}, u32[]{:S(2)}) copy-start(f32[2,1024,8]{1,2,0:T(8,128)S(1)} %divide_subtract_fusion.1) | copy-start | bytes 196612
  284.7 3.7 %copy-start.2 = (bf16[1024,2048]{0,1:T(8,128)(2,1)S(1)}, bf16[1024,2048]{0,1:T(8,128)(2,1)}, u32[]{:S(2)}) copy-start(bf16[1024,2048]{0,1:T(8,128)(2,1)} %copy.92) | copy-start | bytes 12582916
  284.8 4.1 %copy-start.4 = (f32[512,1024]{1,0:T(8,128)S(1)}, f32[512,1024]{1,0:T(8,128)}, u32[]{:S(2)}) copy-start(f32[512,1024]{1,0:T(8,128)} %copy-done.3) | copy-start | bytes 6291460
  284.8 4.3 %copy-start.18 = (bf16[512,1024]{1,0:T(8,128)(2,1)S(1)}, bf16[512,1024]{1,0:T(8,128)(2,1)}, u32[]{:S(2)}) copy-start(bf16[512,1024]{1,0:T(8,128)(2,1)} %param.14) | copy-start | bytes 3145732
  299.6 23.7 %copy-start.12 = (f32[64,128]{1,0:T(8,128)S(1)}, f32[64,128]{1,0:T(8,128)}, u32[]{:S(2)}) copy-start(f32[64,128]{1,0:T(8,128)} %param.21) | copy-start | bytes 98308
  299.6 23.6 %copy-start.13 = (f32[64,128]{1,0:T(8,128)S(1)}, f32[64,128]{1,0:T(8,128)}, u32[]{:S(2)}) copy-start(f32[64,128]{1,0:T(8,128)} %param.22) | copy-start | bytes 98308
  300.6 20.4 %all-to-all-start.1 = ((f32[128,6,128]{2,1,0:T(8,128)}), f32[128,6,128]{2,1,0:T(8,128)S(1)}, u32[]{:S(2)}, u32[]{:S(2)}) async-start(f32[128,6,128]{2,1,0:T(8,128)} %pad_maximum_fusion.1), calls=%async_computation.1 | async-start | bytes 1048576 | tf_op jit(solution)/shard_map/all_to_all | solution.py:116
  323.9 8.2 %copy-start = (f32[64,128]{1,0:T(8,128)}, f32[64,128]{1,0:T(8,128)S(1)}, u32[]{:S(2)}) copy-start(f32[64,128]{1,0:T(8,128)S(1)} %get-tuple-element.43) | copy-start | bytes 98308
  323.9 8.2 %copy-start.5 = (f32[1024,128]{1,0:T(8,128)S(1)}, f32[1024,128]{1,0:T(8,128)}, u32[]{:S(2)}) copy-start(f32[1024,128]{1,0:T(8,128)} %param.23) | copy-start | bytes 1572868
  323.9 8.2 %copy-start.6 = (f32[1024,128]{1,0:T(8,128)S(1)}, f32[1024,128]{1,0:T(8,128)}, u32[]{:S(2)}) copy-start(f32[1024,128]{1,0:T(8,128)} %param.24) | copy-start | bytes 1572868
  325.9 16.6 %all-to-all-start.2 = ((f32[128,4,128]{2,1,0:T(4,128)}), f32[128,4,128]{2,1,0:T(4,128)S(1)}, u32[]{:S(2)}, u32[]{:S(2)}) async-start(f32[128,4,128]{2,1,0:T(4,128)} %broadcast_select_fusion), calls=%async_computation.2 | async-start | bytes 524288 | tf_op jit(solution)/shard_map/all_to_all | solution.py:122
Sparse Core Ops, SparseCore 0:
  11.7 70.5 all-gather.2
  122.4 158.6 all-reduce.3
  284.4 65.2 all-gather.4
where the time goes:
time: 370 us; the launch traced here: 369 us
  waiting for transfers between devices  157 us (42%)
  blocking collectives  68.7 us (19%)
  local copies, waits for them, and re-layouts  64.8 us (18%)
  matrix products  26 us (7%)
  other arithmetic  21.8 us (6%)
  starting transfers between devices  16.7 us (5%)
  between operations  14.3 us (4%)
    unnamed x4, waiting for transfers between devices  82.3 us
    unnamed x1, blocking collectives  68.7 us
    all_gather x2, waiting for transfers between devices, rows_first(): lax.all_gather(both, axis, axis=0, tiled=True)  51.9 us
    gather x2, local copies, waits for them, and re-layouts, local(): jnp.take(slot_values, bag.reshape(-1), axis=0).reshape(samples, -1)  15.8 us
    all_to_all x1, waiting for transfers between devices, local(): lax.all_to_all(packed, 'dev', split_axis=0, concat_axis=0, tiled=True)  13.7 us
    another operation x1, local copies, waits for them, and re-layouts, local(): jnp.stack([weight_one, weight_two])  13.4 us
    gather x2, local copies, waits for them, and re-layouts, local(): jnp.take(held_rows, next_bag.reshape(-1), axis=0)  12.2 us
    all_to_all x1, waiting for transfers between devices, local(): lax.all_to_all(returned, 'dev', split_axis=0, concat_axis=0, tiled=True)  9.17 us
  transfers between devices with their start and end apart: 6, of which 4 were waited for; matrix products, arithmetic and copies ran while one was open for 16% of the time, Pallas kernels for 0%

commit v1 on v0

--- a/solution.py
+++ b/solution.py
@@ -9,10 +9,17 @@
 epsilon = 1e-10
 
 
+def swapped_in(x, mesh_axis, d):
+    peers = lax.axis_size(mesh_axis)
+    parts = jnp.stack([x for _ in range(peers)])
+    parts = lax.all_to_all(parts, mesh_axis, split_axis=0, concat_axis=0)
+    return jnp.concatenate(parts, axis=d)
+
+
 def rows_first(arrays, axis, dims):
     turned = [jnp.moveaxis(a, dim, 0) for a, dim in zip(arrays, dims)]
     both = jnp.concatenate([t.reshape(len(t), -1) for t in turned], axis=1)
-    filled, at, gathered = (lax.all_gather(both, axis, axis=0, tiled=True), 0, [])
+    filled, at, gathered = (swapped_in(both, axis, 0), 0, [])
     for t, dim in zip(turned, dims):
         piece = filled[:, at : at + t[0].size].reshape(-1, *t.shape[1:])
         gathered.append(jnp.moveaxis(piece, 0, dim))

time: 370 us -> 338 us (0.914)
  waiting for transfers between devices: 157 us -> 107 us
  starting transfers between devices: 16.7 us -> 33.2 us
  local copies, waits for them, and re-layouts: 64.8 us -> 68.5 us
    all_to_all x0 -> x2, waiting for transfers between devices: none -> 53.2 us  [swapped_in(): parts = lax.all_to_all(parts, mesh_axis, split_axis=0, concat_axis=0)]
    all_gather x2 -> x0, waiting for transfers between devices: 51.9 us -> none  [rows_first(): lax.all_gather(both, axis, axis=0, tiled=True)]
    unnamed x4 -> x2, waiting for transfers between devices: 82.3 us -> 44.4 us
    all_to_all x0 -> x2, starting transfers between devices: none -> 18.9 us  [swapped_in(): parts = lax.all_to_all(parts, mesh_axis, split_axis=0, concat_axis=0)]
    all_to_all x1, waiting for transfers between devices: 13.7 us -> 0.01 us  [local(): lax.all_to_all(packed, 'dev', split_axis=0, concat_axis=0, tiled=True)]
    all_to_all x1, waiting for transfers between devices: 0.01 us -> 9.27 us  [local(): lax.all_to_all(hot_slots.reshape(devices, -1), 'dev', split_axis=0, conca...]
    all_to_all x1, waiting for transfers between devices: 9.17 us -> 0.01 us  [local(): lax.all_to_all(returned, 'dev', split_axis=0, concat_axis=0, tiled=True)]
    another operation x0 -> x2, local copies, waits for them, and re-layouts: none -> 3.99 us  [swapped_in(): parts = jnp.stack([x for _ in range(peers)])]
  transfers between devices with their start and end apart: 6 -> 6, of which waited for: 4 -> 4; matrix products, arithmetic and copies ran while one was open for 16% -> 17% of each run, Pallas kernels for 0% -> 0%
where the time goes in v1:
time: 338 us; the launch traced here: 337 us
  waiting for transfers between devices  107 us (32%)
  local copies, waits for them, and re-layouts  68.5 us (20%)
  blocking collectives  68.2 us (20%)
  starting transfers between devices  33.2 us (10%)
  matrix products  26.3 us (8%)
  other arithmetic  19.5 us (6%)
  between operations  14.6 us (4%)
    unnamed x1, blocking collectives  68.2 us
    all_to_all x2, waiting for transfers between devices, swapped_in(): parts = lax.all_to_all(parts, mesh_axis, split_axis=0, concat_axis=0)  53.2 us
    unnamed x2, waiting for transfers between devices  44.4 us
    all_to_all x2, starting transfers between devices, swapped_in(): parts = lax.all_to_all(parts, mesh_axis, split_axis=0, concat_axis=0)  18.9 us
    gather x2, local copies, waits for them, and re-layouts, local(): jnp.take(slot_values, bag.reshape(-1), axis=0).reshape(samples, -1)  15.8 us
    another operation x1, local copies, waits for them, and re-layouts, local(): jnp.stack([weight_one, weight_two])  13.4 us
    gather x2, local copies, waits for them, and re-layouts, local(): jnp.take(held_rows, next_bag.reshape(-1), axis=0)  12.3 us
    all_to_all x1, waiting for transfers between devices, local(): lax.all_to_all(hot_slots.reshape(devices, -1), 'dev', split_axis=0, conca...  9.27 us
  transfers between devices with their start and end apart: 6, of which 4 were waited for; matrix products, arithmetic and copies ran while one was open for 17% of the time, Pallas kernels for 0%

profile of v1, /device:TPU:1, one launch (start us, length us, event | category | flops | bytes accessed | tf_op | source)
XLA Modules:
  0.0 337.2 jit_solution(15459773273837228570)
XLA Ops:
  8.8 2.4 stack.16
  11.2 11.9 %all-to-all-start.1 = ((bf16[128,8,2050]{2,1,0:T(8,128)(2,1)}), bf16[128,8,2050]{2,1,0:T(8,128)(2,1)}, u32[]{:S(2)}, u32[]{:S(2)}) async-start(bf16[128,8,2050]{2,1,0:T(8,128)(2,1)} %stack.16), calls=%async_computation.1 | async-start | bytes 8912896 | tf_op jit(solution)/shard_map/all_to_all | solution.py:15
  23.6 14.1 %gather_fusion = f32[4096,128]{1,0:T(8,128)} fusion(f32[768,128]{1,0:T(8,128)S(1)} %pad_maximum_fusion.2, s32[4096]{0:T(1024)S(1)} %broadcast_clamp_fusion.1), kind=kCustom, calls=%fused_computation | custom fusion | bytes 4210688 | tf_op jit(solution)/shard_map/jit(_take)/gather | solution.py:84
  37.7 1.7 gather.21
  39.6 2.7 fusion.9
  42.3 36.3 %all-to-all-done.1 = bf16[128,8,2050]{2,1,0:T(8,128)(2,1)} async-done(((bf16[128,8,2050]{2,1,0:T(8,128)(2,1)}), bf16[128,8,2050]{2,1,0:T(8,128)(2,1)}, u32[]{:S(2)}, u32[]{:S(2)}) %all-to-all-start.1) | async-done | bytes 4198432 | tf_op jit(solution)/shard_map/all_to_all | solution.py:15
  78.6 4.8 %slice.66 = bf16[1024,2048]{1,0:T(8,128)(2,1)} slice(bf16[1024,2050]{1,0:T(8,128)(2,1)} %bitcast.8), slice={[0:1024], [0:2048]} | slice | bytes 8388608 | tf_op jit(solution)/shard_map/slice | solution.py:24
  84.4 6.4 %copy.94 = bf16[1024,2048]{0,1:T(8,128)(2,1)} copy(bf16[1024,2048]{1,0:T(8,128)(2,1)} %slice.66) | data formatting | bytes 8388608 | tf_op jit(solution)/shard_map/reshape | solution.py:24
  91.3 3.3 fusion.11
  94.6 1.6 broadcast_in_dim.51
  96.3 1.7 multiply_reduce_fusion
  99.3 1.7 convolution_bitcast_fusion
  101.0 4.1 %pad_maximum_fusion = f32[2,1024,1024]{2,1,0:T(8,128)} fusion(f32[1,1024,1024]{2,1,0:T(8,128)S(1)} %convolution_bitcast_fusion, f32[1,1024,1024]{2,1,0:T(8,128)S(1)} %convolution_bitcast_fusion.1), kind=kLoop, calls=%fused_computation.7 | loop fusion | flops 2097152 | bytes 16777216 | tf_op jit(solution)/shard_map/stack | solution.py:102
  105.1 13.4 %copy.88 = f32[2,1024,1024]{1,0,2:T(2,128)} copy(f32[2,1024,1024]{2,1,0:T(8,128)} %pad_maximum_fusion) | data formatting | bytes 16777216 | tf_op jit(solution)/shard_map/stack | solution.py:102
  119.9 4.8 %all-to-all-start = ((s32[128,1,4]{2,1,0:T(1,128)}), s32[128,1,4]{2,1,0:T(1,128)S(1)}, u32[]{:S(2)}, u32[]{:S(2)}) async-start(s32[128,1,4]{2,1,0:T(1,128)} %bitcast), calls=%async_computation | async-start | bytes 131072 | tf_op jit(solution)/shard_map/all_to_all | solution.py:119
  124.9 9.3 %all-to-all-done = s32[128,1,4]{2,1,0:T(1,128)S(1)} async-done(((s32[128,1,4]{2,1,0:T(1,128)}), s32[128,1,4]{2,1,0:T(1,128)S(1)}, u32[]{:S(2)}, u32[]{:S(2)}) %all-to-all-start) | async-done | bytes 2080 | tf_op jit(solution)/shard_map/all_to_all | solution.py:119
  135.7 3.8 %fusion.10 = f32[512,1024]{1,0:T(8,128)S(1)} fusion(bf16[2,1024,1024]{2,1,0:T(8,128)(2,1)} %bitcast.104, f32[512,1024]{1,0:T(8,128)} %copy-done.3, f32[512,1024]{1,0:T(8,128)S(1)} %gather.21, pred[64,8,8,128]{3,2,1,0:T(8,128)(4,1)S(1)} %bitcast.101), kind=kOutput, calls=%fused_computation.29 | convolution fusion | flops 1075314688 | bytes 8912896 | tf_op jit(solution)/shard_map/dot_general | solution.py:107
  140.4 5.1 %fusion.4 = bf16[512,1024]{1,0:T(8,128)(2,1)} fusion(f32[512,1024]{1,0:T(8,128)S(1)} %fusion.10, bf16[512,1024]{1,0:T(8,128)(2,1)S(1)} %copy-done.20, f32[512,1024]{1,0:T(8,128)S(1)} %copy-done.4, f32[512,1024]{1,0:T(8,128)} %copy-done.21, bf16[2,1024,1024]{2,1,0:T(8,128)(2,1)S(1)} %bitcast.106, f32[1024]{0:T(1024)S(1)} %get-tuple-element.38, ...), kind=kOutput, calls=%fused_computation.18 | convolution fusion | flops 1081081856 | bytes 15216640 | tf_op jit(solution)/shard_map/dot_general | solution.py:89
  147.1 4.0 %fusion = f32[768,128]{1,0:T(8,128)S(1)} fusion(bf16[4096,128]{1,0:T(8,128)(2,1)S(1)} %reshape.242, s32[4096]{0:T(1024)S(1)} %eq.10), kind=kOutput, calls=%fused_computation.6 | convolution fusion | flops 808452096 | bytes 1458176 | tf_op jit(solution)/shard_map/dot_general | solution.py:113
  152.1 4.6 %all-to-all-start.2 = ((f32[128,6,128]{2,1,0:T(8,128)}), f32[128,6,128]{2,1,0:T(8,128)S(1)}, u32[]{:S(2)}, u32[]{:S(2)}) async-start(f32[128,6,128]{2,1,0:T(8,128)} %pad_maximum_fusion.1), calls=%async_computation.2 | async-start | bytes 1048576 | tf_op jit(solution)/shard_map/all_to_all | solution.py:123
  156.8 68.2 %all-reduce.1 = f32[2,1024]{1,0:T(2,128)S(1)} all-reduce(f32[2,1024]{1,0:T(2,128)S(1)} %pad_maximum_fusion.5), channel_id=3, replica_groups=mesh['dev'=128] {'dev'}, use_global_device_ids=true, to_apply=%region_4.5.clone | all-reduce | flops 2048 | bytes 16384
  225.8 2.3 scatter_custom_fusion
  230.6 4.7 %all-to-all-start.3 = ((f32[128,4,128]{2,1,0:T(4,128)}), f32[128,4,128]{2,1,0:T(4,128)S(1)}, u32[]{:S(2)}, u32[]{:S(2)}) async-start(f32[128,4,128]{2,1,0:T(4,128)} %broadcast_select_fusion), calls=%async_computation.3 | async-start | bytes 524288 | tf_op jit(solution)/shard_map/all_to_all | solution.py:129
  235.4 44.4 %all-reduce.4.cloned.1.call-done = f32[2,1024,1024]{1,0,2:T(2,128)} async-done(((f32[2,1024,1024]{1,0,2:T(2,128)}), f32[2,1024,1024]{1,0,2:T(2,128)}) %all-reduce.4.cloned.1.call-update) | async-done | bytes 8388624
  280.7 1.6 stack.23
  282.4 7.0 %all-to-all-start.4 = ((bf16[128,8,1025]{2,1,0:T(8,128)(2,1)}), bf16[128,8,1025]{2,1,0:T(8,128)(2,1)}, u32[]{:S(2)}, u32[]{:S(2)}) async-start(bf16[128,8,1025]{2,1,0:T(8,128)(2,1)} %stack.23), calls=%async_computation.4 | async-start | bytes 4718592 | tf_op jit(solution)/shard_map/all_to_all | solution.py:15
  290.3 1.6 scatter_custom_fusion.1
  293.1 10.8 %gather_fusion.2 = f32[4096,128]{1,0:T(8,128)S(1)} fusion(f32[512,128]{1,0:T(8,128)S(1)} %bitcast.97, s32[4096]{0:T(1024)S(1)} %broadcast_clamp_fusion), kind=kCustom, calls=%fused_computation.2 | custom fusion | bytes 4210688 | tf_op jit(solution)/shard_map/jit(_take)/gather | solution.py:138
  303.8 1.6 gather.26
  305.4 16.9 %all-to-all-done.4 = bf16[128,8,1025]{2,1,0:T(8,128)(2,1)} async-done(((bf16[128,8,1025]{2,1,0:T(8,128)(2,1)}), bf16[128,8,1025]{2,1,0:T(8,128)(2,1)}, u32[]{:S(2)}, u32[]{:S(2)}) %all-to-all-start.4) | async-done | bytes 2099232 | tf_op jit(solution)/shard_map/all_to_all | solution.py:15
  323.4 1.6 broadcast_in_dim.47
  325.1 5.3 %fusion.6 = bf16[512,1024]{1,0:T(8,128)(2,1)} fusion(f32[512,1024]{1,0:T(8,128)} %gather.26, pred[64,8,8,128]{3,2,1,0:T(8,128)(4,1)S(1)} %bitcast.111, bf16[1024,1025]{1,0:T(8,128)(2,1)} %bitcast.28, f32[1024]{0:T(1024)S(1)} %convert_reduce_fusion), kind=kOutput, calls=%fused_computation.20 | convolution fusion | flops 1077411840 | bytes 8392704 | tf_op jit(solution)/shard_map/dot_general | solution.py:139
  (98 shorter events, 18.9 us)
Async XLA Ops:
  11.2 12.0 %copy-start.11 = (s32[512,8]{0,1:T(8,128)S(1)}, s32[512,8]{0,1:T(8,128)}, u32[]{:S(2)}) copy-start(s32[512,8]{0,1:T(8,128)} %param.15) | copy-start | bytes 49156
  11.2 12.3 %copy-start.7 = (f32[512,128]{1,0:T(8,128)S(1)}, f32[512,128]{1,0:T(8,128)}, u32[]{:S(2)}) copy-start(f32[512,128]{1,0:T(8,128)} %param.19) | copy-start | bytes 786436
  11.2 12.3 %copy-start.9 = (f32[256,128]{1,0:T(8,128)S(1)}, f32[256,128]{1,0:T(8,128)}, u32[]{:S(2)}) copy-start(f32[256,128]{1,0:T(8,128)} %param.20) | copy-start | bytes 393220
  11.2 67.4 %all-to-all-start.1 = ((bf16[128,8,2050]{2,1,0:T(8,128)(2,1)}), bf16[128,8,2050]{2,1,0:T(8,128)(2,1)}, u32[]{:S(2)}, u32[]{:S(2)}) async-start(bf16[128,8,2050]{2,1,0:T(8,128)(2,1)} %stack.16), calls=%async_computation.1 | async-start | bytes 8912896 | tf_op jit(solution)/shard_map/all_to_all | solution.py:15
  23.1 256.7 %all-reduce.4.cloned.1.call-start = ((), (), s32[]{:S(2)}) async-start(), calls=%async_computation.5 | async-start | bytes 16777216
  91.3 5.0 %copy-start.1 = (bf16[1024,2048]{0,1:T(8,128)(2,1)S(1)}, bf16[1024,2048]{0,1:T(8,128)(2,1)}, u32[]{:S(2)}) copy-start(bf16[1024,2048]{0,1:T(8,128)(2,1)} %copy.94) | copy-start | bytes 12582916
  91.3 5.0 %copy-start.19 = (bf16[512,1024]{1,0:T(8,128)(2,1)S(1)}, bf16[512,1024]{1,0:T(8,128)(2,1)}, u32[]{:S(2)}) copy-start(bf16[512,1024]{1,0:T(8,128)(2,1)} %param.14) | copy-start | bytes 3145732
  94.6 4.7 %copy-start.21 = (f32[512,1024]{1,0:T(8,128)}, f32[512,1024]{1,0:T(8,128)S(1)}, u32[]{:S(2)}) copy-start(f32[512,1024]{1,0:T(8,128)S(1)} %fusion.11) | copy-start | bytes 6291460
  97.9 1.4 copy-start.3
  118.5 0.7 copy-start.16
  119.9 14.3 %all-to-all-start = ((s32[128,1,4]{2,1,0:T(1,128)}), s32[128,1,4]{2,1,0:T(1,128)S(1)}, u32[]{:S(2)}, u32[]{:S(2)}) async-start(s32[128,1,4]{2,1,0:T(1,128)} %bitcast), calls=%async_computation | async-start | bytes 131072 | tf_op jit(solution)/shard_map/all_to_all | solution.py:119
  135.7 3.9 %copy-start.2 = (bf16[1024,2048]{0,1:T(8,128)(2,1)S(1)}, bf16[1024,2048]{0,1:T(8,128)(2,1)}, u32[]{:S(2)}) copy-start(bf16[1024,2048]{0,1:T(8,128)(2,1)} %copy.94) | copy-start | bytes 12582916
  135.7 4.5 %copy-start.4 = (f32[512,1024]{1,0:T(8,128)S(1)}, f32[512,1024]{1,0:T(8,128)}, u32[]{:S(2)}) copy-start(f32[512,1024]{1,0:T(8,128)} %copy-done.3) | copy-start | bytes 6291460
  135.7 4.7 %copy-start.20 = (bf16[512,1024]{1,0:T(8,128)(2,1)S(1)}, bf16[512,1024]{1,0:T(8,128)(2,1)}, u32[]{:S(2)}) copy-start(bf16[512,1024]{1,0:T(8,128)(2,1)} %param.14) | copy-start | bytes 3145732
  151.1 73.9 %copy-start.18 = (f32[2,8]{1,0:T(2,128)S(1)}, f32[2,8]{1,0:T(2,128)}, u32[]{:S(2)}) copy-start(f32[2,8]{1,0:T(2,128)} %param.26) | copy-start | bytes 196
  151.1 76.9 %copy-start.14 = (f32[64,128]{1,0:T(8,128)S(1)}, f32[64,128]{1,0:T(8,128)}, u32[]{:S(2)}) copy-start(f32[64,128]{1,0:T(8,128)} %param.21) | copy-start | bytes 98308
  151.1 76.9 %copy-start.15 = (f32[64,128]{1,0:T(8,128)S(1)}, f32[64,128]{1,0:T(8,128)}, u32[]{:S(2)}) copy-start(f32[64,128]{1,0:T(8,128)} %param.22) | copy-start | bytes 98308
  152.1 73.6 %all-to-all-start.2 = ((f32[128,6,128]{2,1,0:T(8,128)}), f32[128,6,128]{2,1,0:T(8,128)S(1)}, u32[]{:S(2)}, u32[]{:S(2)}) async-start(f32[128,6,128]{2,1,0:T(8,128)} %pad_maximum_fusion.1), calls=%async_computation.2 | async-start | bytes 1048576 | tf_op jit(solution)/shard_map/all_to_all | solution.py:123
  225.7 54.9 %copy-start.8 = (f32[2,1024,8]{1,2,0:T(8,128)S(1)}, f32[2,1024,8]{1,2,0:T(8,128)}, u32[]{:S(2)}) copy-start(f32[2,1024,8]{1,2,0:T(8,128)} %param.25) | copy-start | bytes 196612
  225.7 54.9 %copy-start.13 = (f32[2,1024,8]{1,2,0:T(8,128)S(1)}, f32[2,1024,8]{1,2,0:T(8,128)}, u32[]{:S(2)}) copy-start(f32[2,1024,8]{1,2,0:T(8,128)} %param.27) | copy-start | bytes 196612
  228.7 53.6 %copy-start = (f32[64,128]{1,0:T(8,128)}, f32[64,128]{1,0:T(8,128)S(1)}, u32[]{:S(2)}) copy-start(f32[64,128]{1,0:T(8,128)S(1)} %get-tuple-element.43) | copy-start | bytes 98308
  230.6 50.1 %all-to-all-start.3 = ((f32[128,4,128]{2,1,0:T(4,128)}), f32[128,4,128]{2,1,0:T(4,128)S(1)}, u32[]{:S(2)}, u32[]{:S(2)}) async-start(f32[128,4,128]{2,1,0:T(4,128)} %broadcast_select_fusion), calls=%async_computation.3 | async-start | bytes 524288 | tf_op jit(solution)/shard_map/all_to_all | solution.py:129
  280.7 1.6 copy-start.10
  282.3 7.1 %copy-start.12 = (s32[512,8]{0,1:T(8,128)S(1)}, s32[512,8]{0,1:T(8,128)}, u32[]{:S(2)}) copy-start(s32[512,8]{0,1:T(8,128)} %param.16) | copy-start | bytes 49156
  282.3 7.6 %copy-start.17 = (s32[1,128,2]{1,2,0:T(2,128)S(1)}, s32[1,128,2]{1,2,0:T(2,128)}, u32[]{:S(2)}) copy-start(s32[1,128,2]{1,2,0:T(2,128)} %param.18) | copy-start | bytes 3076
  282.3 9.5 %copy-start.5 = (f32[1024,128]{1,0:T(8,128)S(1)}, f32[1024,128]{1,0:T(8,128)}, u32[]{:S(2)}) copy-start(f32[1024,128]{1,0:T(8,128)} %param.23) | copy-start | bytes 1572868
  282.3 9.5 %copy-start.6 = (f32[1024,128]{1,0:T(8,128)S(1)}, f32[1024,128]{1,0:T(8,128)}, u32[]{:S(2)}) copy-start(f32[1024,128]{1,0:T(8,128)} %param.24) | copy-start | bytes 1572868
  282.4 40.0 %all-to-all-start.4 = ((bf16[128,8,1025]{2,1,0:T(8,128)(2,1)}), bf16[128,8,1025]{2,1,0:T(8,128)(2,1)}, u32[]{:S(2)}, u32[]{:S(2)}) async-start(bf16[128,8,1025]{2,1,0:T(8,128)(2,1)} %stack.23), calls=%async_computation.4 | async-start | bytes 4718592 | tf_op jit(solution)/shard_map/all_to_all | solution.py:15
Sparse Core Ops, SparseCore 0:
  118.6 161.0 all-reduce.3
